TPU v7x, 32 devices: a whole 2x2x4 slice. The times are simulated.
32 devices in a mesh: tm: 16 (over z, y, core), col: 2 (over x).
Axes of the slice: x: 2, y: 2, z: 4, core: 2. Of those that a mesh axis runs over, the one named last changes fastest.
Arguments:
- design: bfloat16 [2048, 2, 512], P('tm', None, 'col'), may hold values from -512 to 512
- filter_taps: bfloat16 [16, 2, 512], replicated, may hold values from -3 to 3
- segment: int32 [2048], P('tm'), may hold values from 0 to 15, never falling along the last dimension, each value on 1 to 256 neighbouring positions
- valid_flags: int32 [2048], P('tm'), may hold values 0 or 1
- weights: float32 [2, 2048], P(None, 'tm'), may hold values from 0.05 to 20
- block_ids: int32 [2], replicated, may hold values from 0 to 1, each once
Outputs:
- normals: float32 [512, 512], P('tm', 'col')
All inputs are finite; a program needn't handle non-finite values. No bound on the sum of `valid_flags` on one device may be relied on, other than what follows from the above.
Results may differ from a plain program's by a relative error of at most 0.0013.
Values may be sent and summed in bfloat16 or wider, within the bound.
No kernel may reach another device: no remote copies, remote signals or barrier semaphores. Data moves between devices by JAX's collectives and lax.ppermute only.
A program may use at most 64 MiB of HBM per device.

v0:
```python
import functools

import jax
import jax.numpy as jnp
from jax import lax
from jax.experimental import pallas as pl
from jax.experimental.pallas import tpu as pltpu
from jax.sharding import PartitionSpec as P

VMEM = pl.BlockSpec(memory_space=pltpu.VMEM)
SMEM = pl.BlockSpec(memory_space=pltpu.SMEM)
FIRST = (((0,), (0,)), ((), ()))
LIMIT = pltpu.CompilerParams(vmem_limit_bytes=24 * 2**20)


def rows_kernel(weights_ref, flags_ref, segment_ref, rows_ref):
    rows_ref[0:2, :] = weights_ref[...] * flags_ref[...].astype(jnp.float32)
    rows_ref[2:3, :] = segment_ref[...].astype(jnp.float32)
    rows_ref[3:, :] = jnp.zeros_like(rows_ref[3:, :])


def prepare_kernel(taps_ref, design_ref, spread_ref, own_ref):
    own_ref[...] = design_ref[...]
    seg_count, _, tap_count = taps_ref.shape
    width = spread_ref.shape[1]
    row_count = design_ref.shape[0]
    tile = 128
    lane = lax.broadcasted_iota(jnp.int32, (tile, 2 * tile), 1)
    row = lax.broadcasted_iota(jnp.int32, (tile, 2 * tile), 0)
    taps = taps_ref[...].reshape(2 * seg_count, tap_count)
    component = lax.rem(lax.broadcasted_iota(jnp.int32, (2 * seg_count, 2 * tile), 0), 2)
    flips = [(lane == 2 * (tile - 1 - row) + k).astype(jnp.float32).astype(jnp.bfloat16) for k in range(2)]
    pieces = []
    for place in range(tap_count - tile, -1, -tile):
        part = taps[:, place : place + tile]
        first, second = (jnp.dot(part, flip, preferred_element_type=jnp.float32) for flip in flips)
        pieces.append(jnp.where(component == 0, first, second))
    pieces.append(jnp.zeros((2 * seg_count, width - 2 * tap_count), jnp.float32))
    spread = pltpu.roll(jnp.concatenate(pieces, axis=1), width - 2 * row_count - 2 * (tap_count - 1), 1)
    spread_ref[...] = spread.astype(jnp.bfloat16)


def choose_kernel(rows_across_ref, across_ref, own_ref, beside_ref, out_ref):
    out_ref[1] = beside_ref[...]
    index = lax.axis_index("tm")
    both = jnp.bitwise_and(jnp.bitwise_xor(index, lax.div(index, 2)), 1)

    @pl.when(both == 0)
    def _():
        out_ref[0] = across_ref[...]

    @pl.when(both == 1)
    def _():
        out_ref[0] = own_ref[...]


def toeplitz_kernel(rows_ref, rows_across_ref, spread_ref, out_ref, rows_here_ref):
    sources, width = spread_ref.shape
    depth, _, step = out_ref.shape
    row_count = step // 2
    later, epoch_block = epoch_block_here()
    rows = jnp.where(later, rows_across_ref[...], rows_ref[...])
    rows_here_ref[...] = rows
    segment = 2 * rows[2:3, :].astype(jnp.int32)
    source = lax.broadcasted_iota(jnp.int32, (sources, row_count), 0)
    column = lax.broadcasted_iota(jnp.int32, (row_count, width), 1)
    first_column = 2 * ((depth - 1) - epoch_block) * row_count
    for k in range(2):
        selector = (source == segment + k).astype(jnp.float32).astype(jnp.bfloat16)
        shifted = lax.dot_general(selector, spread_ref[...], FIRST, preferred_element_type=jnp.float32)
        shifted = pltpu.roll(shifted, 0, 1, stride=2, stride_axis=0)
        shifted = jnp.where(column >= first_column, shifted, 0.0).astype(jnp.bfloat16)
        for d in range(depth):
            place = (depth - 1 - d) * step
            out_ref[d, k * row_count : (k + 1) * row_count, :] = shifted[:, place : place + step]


def epoch_block_here():
    index, devices = lax.axis_index("tm"), lax.axis_size("tm")
    later = lax.rem(lax.div(index, 2), 2) == 0
    return later, jnp.where(later, lax.rem(index + 4, devices), index)


def filtered_block(toeplitz_ref, across_ref, own_ref, beside_ref, swapped_ref):
    row_count, _, width = own_ref.shape
    step = 2 * row_count
    later, _ = epoch_block_here()
    odd = lax.rem(lax.axis_index("tm"), 2)
    back = jnp.where(later, 4, 0)
    total = None
    for d, block_ref in (
        (2, beside_ref),
        (1 + 2 * odd, swapped_ref.at[1]),
        (back, own_ref),
        (4 - back, across_ref),
        (3 - 2 * odd, swapped_ref.at[0]),
    ):
        product = jnp.dot(
            toeplitz_ref[d], block_ref[...].reshape(step, width), preferred_element_type=jnp.float32
        )
        total = product if total is None else total + product
    return total.T.astype(jnp.bfloat16)


def filter_kernel(toeplitz_ref, across_ref, own_ref, beside_ref, swapped_ref, out_ref):
    block = filtered_block(toeplitz_ref, across_ref, own_ref, beside_ref, swapped_ref)
    out_ref[...] = block.reshape(out_ref.shape)


def filter_split_kernel(
    toeplitz_ref, across_ref, own_ref, beside_ref, swapped_ref, rows_ref, all_ref, here_ref, there_ref
):
    block = filtered_block(toeplitz_ref, across_ref, own_ref, beside_ref, swapped_ref)
    width, length = block.shape
    all_ref[0:width, :] = block
    weight = jnp.concatenate([rows_ref[0:1], rows_ref[1:2]], axis=1)
    high = weight.astype(jnp.bfloat16).astype(jnp.float32)
    middle = (weight - high).astype(jnp.bfloat16).astype(jnp.float32)
    low = weight - high - middle
    line = lax.broadcasted_iota(jnp.int32, (all_ref.shape[0] - width, length), 0)
    spread = jnp.where(line == 0, high, jnp.where(line == 1, middle, jnp.where(line == 2, low, 0.0)))
    all_ref[width:, :] = spread.astype(jnp.bfloat16)
    groups, _, rows_out, _ = here_ref.shape
    block = block.reshape(groups, 2, 2, rows_out, length)
    place = lax.rem(lax.div(lax.axis_index("tm"), 2), 2)
    for side in range(2):

        @pl.when(place == side)
        def _(side=side):
            here_ref[...] = block[:, side]
            there_ref[...] = block[:, 1 - side]


def split_scale_kernel(*refs):
    *held_refs, other_ref, scaled_ref = refs
    held_refs = [held_refs[i] for i in (3, 2, 1, 0)]
    width = scaled_ref.shape[1]
    for unit, ref in enumerate(held_refs[:2]):
        lines = ref[width:, :].astype(jnp.float32)
        weight = lines[0:1] + lines[1:2] + lines[2:3]
        scaled_ref[unit] = (ref[0:width, :].astype(jnp.float32) * weight).astype(jnp.bfloat16)
    split_gram(held_refs, scaled_ref, other_ref, 1)


def split_gram_kernel(scaled_ref, *refs):
    *held_refs, mine_ref = refs
    held_refs = [held_refs[i] for i in (3, 2, 1, 0)]
    split_gram(held_refs, scaled_ref, mine_ref, 0)


def split_gram(held_refs, scaled_ref, out_ref, flip):
    index, column = lax.axis_index("tm"), lax.axis_index("col")
    place = lax.rem(lax.div(index, 2), 2)
    parity = jnp.bitwise_xor(lax.rem(index, 2), flip)
    all_refs, half_refs = held_refs[:2], held_refs[2:]
    groups, _, rows_out, length = half_refs[0].shape
    first = place * 2 * rows_out + parity * rows_out
    for block in range(2):
        total = None
        for unit in range(2):
            if block == 0:
                pieces = [
                    all_refs[unit][pl.ds(pl.multiple_of(g * 4 * rows_out + first, rows_out), rows_out), :]
                    for g in range(groups)
                ]
                rows = jnp.concatenate(pieces, axis=0)
            else:
                rows = half_refs[unit][:, parity].reshape(groups * rows_out, length)
            product = lax.dot_general(
                rows, scaled_ref[unit], (((1,), (1,)), ((), ())), preferred_element_type=jnp.float32
            )
            total = product if total is None else total + product
        at = jnp.bitwise_xor(column, block) * groups
        out_ref[pl.ds(at, groups)] = total.reshape(groups, rows_out, total.shape[1])


def scale_kernel(ids_ref, rows_ref, rows_beside_ref, *refs):
    *held_refs, other_ref, scaled_ref = refs
    columns = len(held_refs) // 2
    width, length = scaled_ref.shape[1:]
    column = lax.axis_index("col")
    for unit, ref in enumerate((rows_ref, rows_beside_ref)):
        weight = jnp.concatenate([ref[0:1], ref[1:2]], axis=1)
        for d in range(columns):

            @pl.when(ids_ref[lax.rem(column + d, columns)] == column)
            def _(d=d, unit=unit, weight=weight):
                values = held_refs[2 * d + unit][...].reshape(width, length).astype(jnp.float32)
                scaled_ref[unit] = (values * weight).astype(jnp.bfloat16)

    gram(ids_ref, held_refs, scaled_ref, other_ref, 1)


def gram_kernel(ids_ref, scaled_ref, *refs):
    *held_refs, mine_ref = refs
    gram(ids_ref, held_refs, scaled_ref, mine_ref, 0)


def gram(ids_ref, held_refs, scaled_ref, out_ref, flip):
    columns = len(held_refs) // 2
    index, column = lax.axis_index("tm"), lax.axis_index("col")
    beside = lax.rem(lax.div(index, 2), 2)
    parity = jnp.bitwise_xor(lax.rem(index, 2), flip)
    length = scaled_ref.shape[2]
    groups, _, _, rows_out, _ = held_refs[0].shape
    for d in range(columns):
        total = None
        for unit in range(2):
            rows = held_refs[2 * d + unit][:, beside, parity].reshape(groups * rows_out, length)
            product = lax.dot_general(
                rows, scaled_ref[unit], (((1,), (1,)), ((), ())), preferred_element_type=jnp.float32
            )
            total = product if total is None else total + product
        place = pl.ds(ids_ref[lax.rem(column + d, columns)] * groups, groups)
        out_ref[place] = total.reshape(groups, rows_out, total.shape[1])


def body(design, filter_taps, segment, valid_flags, weights, block_ids):
    row_count = design.shape[0]
    block_width = design.shape[2]
    tap_count = filter_taps.shape[2]
    seg_count = filter_taps.shape[0]
    devices = lax.axis_size("tm")
    columns = lax.axis_size("col")
    rows_out = columns * block_width // devices
    halo_depth = (tap_count - 2) // row_count + 1
    if halo_depth != 4 or devices % 4:
        raise ValueError("halo depth")
    index = lax.axis_index("tm")
    swap = [(i, i ^ 1) for i in range(devices)]
    beside_pairs = [(i, i ^ 2) for i in range(devices)]
    across_pairs = [(i, (i + (4 if i & 2 else -4)) % devices) for i in range(devices)]

    across = lax.ppermute(design, "tm", across_pairs)
    rows = pl.pallas_call(
        rows_kernel,
        out_shape=jax.ShapeDtypeStruct((8, row_count), jnp.float32),
        in_specs=[VMEM] * 3,
        out_specs=VMEM,
        compiler_params=LIMIT,
        name="rows",
    )(weights, valid_flags.reshape(1, row_count), segment.reshape(1, row_count))
    rows_pairs = [(i, i ^ 4 if i & 2 else (i - 4) % devices) for i in range(devices)]
    rows_across = lax.ppermute(rows, "tm", rows_pairs)
    beside = lax.ppermute(design, "tm", beside_pairs)
    spread, own = pl.pallas_call(
        prepare_kernel,
        out_shape=[
            jax.ShapeDtypeStruct((2 * seg_count, 2 * (halo_depth + 1) * row_count), jnp.bfloat16),
            jax.ShapeDtypeStruct(design.shape, design.dtype),
        ],
        in_specs=[VMEM] * 2,
        out_specs=[VMEM] * 2,
        compiler_params=LIMIT,
        name="prepare",
    )(filter_taps, design)
    toeplitz, rows_here = pl.pallas_call(
        toeplitz_kernel,
        out_shape=[
            jax.ShapeDtypeStruct((halo_depth + 1, 2 * row_count, 2 * row_count), jnp.bfloat16),
            jax.ShapeDtypeStruct(rows.shape, rows.dtype),
        ],
        in_specs=[VMEM] * 3,
        out_specs=[VMEM] * 2,
        compiler_params=LIMIT,
        name="toeplitz",
    )(rows, rows_across, spread)
    chosen = pl.pallas_call(
        choose_kernel,
        out_shape=jax.ShapeDtypeStruct((2, *design.shape), design.dtype),
        in_specs=[VMEM] * 4,
        out_specs=VMEM,
        compiler_params=LIMIT,
        name="choose",
    )(rows_across, across, own, beside)
    swapped = lax.ppermute(chosen, "tm", swap)
    split = columns == 2 and rows_out % 16 == 0 and block_width % (4 * rows_out) == 0
    finish = finish_two if split else finish_any
    total = finish(toeplitz, rows_here, (across, own, beside, swapped), block_ids, rows_out, swap, beside_pairs)
    return total * (1.0 / (2.0 * row_count * devices))


def core_sum(mine, other, swap):
    return mine + lax.ppermute(other, "tm", swap)


def sum_over_groups(total, stride):
    devices = lax.axis_size("tm")
    index = lax.axis_index("tm")
    left = total.shape[0]
    while left > 1:
        group = 4 if left % 4 == 0 else 2
        shares = total.reshape(left // group, group, *total.shape[1:])
        place = index // stride % group

        def share(j):
            return lax.dynamic_index_in_dim(shares, j, 1, keepdims=False)

        total = share(place)
        for d in (2, 3, 1)[-(group - 1) :]:
            total = total + lax.ppermute(share(place ^ d), "tm", [(i, i ^ (d * stride)) for i in range(devices)])
        stride, left = stride * group, left // group
    return total[0]


def finish_two(toeplitz, rows_here, blocks, block_ids, rows_out, swap, beside_pairs):
    devices = lax.axis_size("tm")
    length, width = toeplitz.shape[1], blocks[0].shape[2]
    groups = width // rows_out // 4
    half = jax.ShapeDtypeStruct((groups, 2, rows_out, length), jnp.bfloat16)
    every, here, there = pl.pallas_call(
        filter_split_kernel,
        out_shape=[jax.ShapeDtypeStruct((width + 16, length), jnp.bfloat16), half, half],
        in_specs=[VMEM] * 6,
        out_specs=[VMEM] * 3,
        compiler_params=LIMIT,
        name="filter",
    )(toeplitz, *blocks, rows_here)

    def sums(own_block):
        def run(every, here, there):
            across_column = [(0, 1), (1, 0)]
            both = [(i * 2 + c, (i ^ 2) * 2 + 1 - c) for i in range(devices) for c in range(2)]
            if own_block:
                held = (
                    every,
                    lax.ppermute(every, "tm", beside_pairs),
                    lax.ppermute(here, "col", across_column),
                    lax.ppermute(there, ("tm", "col"), both),
                )
            else:
                held = (
                    lax.ppermute(every, "col", across_column),
                    lax.ppermute(every, ("tm", "col"), both),
                    here,
                    lax.ppermute(there, "tm", beside_pairs),
                )
            share = jax.ShapeDtypeStruct((2 * groups, rows_out, width), jnp.float32)
            other, scaled = pl.pallas_call(
                split_scale_kernel,
                out_shape=[share, jax.ShapeDtypeStruct((2, width, length), jnp.bfloat16)],
                in_specs=[VMEM] * 4,
                out_specs=[VMEM] * 2,
                compiler_params=LIMIT,
                name="scale",
            )(*(held[i] for i in (3, 2, 1, 0)))
            mine = pl.pallas_call(
                split_gram_kernel,
                out_shape=share,
                in_specs=[VMEM] * 5,
                out_specs=VMEM,
                compiler_params=LIMIT,
                name="gram",
            )(scaled, *(held[i] for i in (3, 2, 1, 0)))
            return sum_over_groups(core_sum(mine, other, swap), 4)

        return run

    return lax.cond(block_ids[0] == 0, sums(True), sums(False), every, here, there)


def finish_any(toeplitz, rows_here, blocks, block_ids, rows_out, swap, beside_pairs):
    devices, columns = lax.axis_size("tm"), lax.axis_size("col")
    length, width = toeplitz.shape[1], blocks[0].shape[2]
    filtered = pl.pallas_call(
        filter_kernel,
        out_shape=jax.ShapeDtypeStruct((width // rows_out // 4, 2, 2, rows_out, length), jnp.bfloat16),
        in_specs=[VMEM] * 5,
        out_specs=VMEM,
        compiler_params=LIMIT,
        name="filter",
    )(toeplitz, *blocks)
    held = []
    for d in range(columns):
        for e in range(2):
            pairs = [
                (i * columns + (c + d) % columns, (i ^ 2 * e) * columns + c)
                for i in range(devices)
                for c in range(columns)
            ]
            held.append(lax.ppermute(filtered, ("tm", "col"), pairs) if d or e else filtered)
    rows_beside = lax.ppermute(rows_here, "tm", beside_pairs)
    share = jax.ShapeDtypeStruct((devices // 4, rows_out, width), jnp.float32)
    other, scaled = pl.pallas_call(
        scale_kernel,
        out_shape=[share, jax.ShapeDtypeStruct((2, width, length), jnp.bfloat16)],
        in_specs=[SMEM] + [VMEM] * (2 + 2 * columns),
        out_specs=[VMEM] * 2,
        compiler_params=LIMIT,
        name="scale",
    )(block_ids, rows_here, rows_beside, *held)
    mine = pl.pallas_call(
        gram_kernel,
        out_shape=share,
        in_specs=[SMEM] + [VMEM] * (1 + 2 * columns),
        out_specs=VMEM,
        compiler_params=LIMIT,
        name="gram",
    )(block_ids, scaled, *held)
    return sum_over_groups(core_sum(mine, other, swap), 4)


def solution(mesh):
    return jax.shard_map(
        body,
        mesh=mesh,
        in_specs=(P("tm", None, "col"), P(), P("tm"), P("tm"), P(None, "tm"), P()),
        out_specs=P("tm", "col"),
        check_vma=False,
    )
```

profile of v0, /device:TPU:0, one launch (start us, length us, event | category | flops | bytes accessed | tf_op | source)
XLA Modules:
  0.0 31.2 jit_solution(11350294857367256641)
XLA Ops:
  0.0 5.0 %collective-permute-start.15 = (bf16[128,2,256]{2,1,0:T(2,128)(2,1)}, bf16[128,2,256]{2,1,0:T(2,128)(2,1)S(1)}, u32[]{:S(2)}, u32[]{:S(2)}) collective-permute-start(bf16[128,2,256]{2,1,0:T(2,128)(2,1)} %design_ref.1), channel_id=1, source_target_pairs={{0,24},{2,26},{4,12},{6,14},{8,0},{10,2},{12,20},{14,22},{16,8},{1... | collective-permute-start | bytes 393224 | tf_op jit(solution)/shard_map/ppermute | solution.py:234
  5.1 0.6 %copy-done.4 = s32[128]{0:T(128)S(1)} copy-done((s32[128]{0:T(128)S(1)}, s32[128]{0:T(128)}, u32[]{:S(2)}) %copy-start.4) | copy-done | bytes 536
  5.7 0.0 copy-done.2
  5.8 1.8 %collective-permute-start.14 = (f32[8,128]{1,0:T(8,128)S(1)}, f32[8,128]{1,0:T(8,128)S(1)}, u32[]{:S(2)}, u32[]{:S(2)}) collective-permute-start(f32[8,128]{1,0:T(8,128)S(1)} %rows.1.rows_ref), channel_id=1, source_target_pairs={{0,24},{2,26},{4,12},{6,14},{8,0},{10,2},{12,4},{14,6},{16,8},{18,... | collective-permute-start | bytes 12296 | tf_op jit(solution)/shard_map/ppermute | solution.py:244
  7.5 0.9 %copy-done = bf16[128,2,256]{2,1,0:T(2,128)(2,1)S(1)} copy-done((bf16[128,2,256]{2,1,0:T(2,128)(2,1)S(1)}, bf16[128,2,256]{2,1,0:T(2,128)(2,1)}, u32[]{:S(2)}) %copy-start) | copy-done | bytes 131096
  8.4 0.8 %copy-done.1 = bf16[16,2,512]{2,1,0:T(2,128)(2,1)S(1)} copy-done((bf16[16,2,512]{2,1,0:T(2,128)(2,1)S(1)}, bf16[16,2,512]{2,1,0:T(2,128)(2,1)}, u32[]{:S(2)}) %copy-start.1) | copy-done | bytes 32792
  9.2 0.3 prepare.1
  9.5 0.0 collective-permute-done.14.rows_across_ref
  9.5 0.7 %collective-permute-done.16.beside_ref = bf16[128,2,256]{2,1,0:T(2,128)(2,1)S(1)} collective-permute-done((bf16[128,2,256]{2,1,0:T(2,128)(2,1)}, bf16[128,2,256]{2,1,0:T(2,128)(2,1)S(1)}, u32[]{:S(2)}, u32[]{:S(2)}) %collective-permute-start.16) | collective-permute-done | bytes 131104 | tf_op jit(solution)/shard_map/ppermute | solution.py:245
  10.3 0.0 copy-start.5
  10.3 0.1 collective-permute-start.17
  10.4 0.6 %copy-done.5 = s32[2]{0:T(128)S(1)} copy-done((s32[2]{0:T(128)S(1)}, s32[2]{0:T(128)}, u32[]{:S(2)}) %copy-start.5) | copy-done | bytes 32
  11.0 0.5 %toeplitz.1 = (bf16[5,256,256]{2,1,0:T(8,128)(2,1)S(1)}, f32[8,128]{1,0:T(8,128)S(1)}) custom-call(f32[8,128]{1,0:T(8,128)S(1)} %rows.1.rows_ref, f32[8,128]{1,0:T(8,128)S(1)} %collective-permute-done.14.rows_across_ref, bf16[32,1280]{1,0:T(8,128)(2,1)S(1)} %get-tuple-element.37.spread_ref), custom_call_target="tpu_custom_call" | custom-call | tf_op jit(solution)/shard_map/toeplitz/pallas_call | solution.py:257
  11.5 0.4 %collective-permute-done.17.swapped_ref = bf16[2,128,2,256]{3,2,1,0:T(2,128)(2,1)S(1)} collective-permute-done((bf16[2,128,2,256]{3,2,1,0:T(2,128)(2,1)S(1)}, bf16[2,128,2,256]{3,2,1,0:T(2,128)(2,1)S(1)}, u32[]{:S(2)}, u32[]{:S(2)}) %collective-permute-start.17) | collective-permute-done | bytes 262176 | tf_op jit(solution)/shard_map/ppermute | solution.py:276
  11.9 0.5 %filter.1 = (bf16[272,256]{1,0:T(8,128)(2,1)S(1)}, bf16[2,2,32,256]{3,2,1,0:T(8,128)(2,1)S(1)}, bf16[2,2,32,256]{3,2,1,0:T(8,128)(2,1)S(1)}) custom-call(bf16[5,256,256]{2,1,0:T(8,128)(2,1)S(1)} %get-tuple-element.38.toeplitz_ref, bf16[128,2,256]{2,1,0:T(2,128)(2,1)S(1)} %collective-permute-done.15.across_ref, ...), custom_call_target="tpu_custom_call" | custom-call | tf_op jit(solution)/shard_map/filter/pallas_call | solution.py:311
  12.4 18.2 %conditional.1 = (f32[32,256]{1,0:T(8,128)S(1)}) conditional(s32[]{:T(128)} %bitcast.2, (bf16[2,2,32,256]{3,2,1,0:T(8,128)(2,1)S(1)}, bf16[272,256]{1,0:T(8,128)(2,1)S(1)}, bf16[2,2,32,256]{3,2,1,0:T(8,128)(2,1)S(1)}) %tuple.11, (bf16[2,2,32,256]{3,2,1,0:T(8,128)(2,1)S(1)}, bf16[2,2,32,256]{3,2,1,0:T(8,128)(2,1)S(1)}, ...), branch_computations={%region_0.1_spmd, %region_1.2_spmd} | conditional | flops 57388 | bytes 3048191 | solution.py:359
  12.4 2.2 %collective-permute-start.1 = (bf16[272,256]{1,0:T(8,128)(2,1)S(1)}, bf16[272,256]{1,0:T(8,128)(2,1)S(1)}, u32[]{:S(2)}, u32[]{:S(2)}) collective-permute-start(bf16[272,256]{1,0:T(8,128)(2,1)S(1)} %get-tuple-element.22), channel_id=1, source_target_pairs={{0,5},{1,4},{2,7},{3,6},{4,1},{5,0},{6,3},{7,2},{8,13},{9,12},{10,... | collective-permute-start | bytes 417800 | tf_op jit(solution)/shard_map/cond/branch_0_fun/ppermute | solution.py:334
  14.6 0.5 %collective-permute-start.2 = (bf16[272,256]{1,0:T(8,128)(2,1)S(1)}, bf16[272,256]{1,0:T(8,128)(2,1)S(1)}, u32[]{:S(2)}, u32[]{:S(2)}) collective-permute-start(bf16[272,256]{1,0:T(8,128)(2,1)S(1)} %get-tuple-element.22), channel_id=1, source_target_pairs={{0,1},{1,0},{2,3},{3,2},{4,5},{5,4},{6,7},{7,6},{8,9},{9,8},{10,11... | collective-permute-start | bytes 417800 | tf_op jit(solution)/shard_map/cond/branch_0_fun/ppermute | solution.py:333
  15.1 0.8 %collective-permute-start = (bf16[2,2,32,256]{3,2,1,0:T(8,128)(2,1)S(1)}, bf16[2,2,32,256]{3,2,1,0:T(8,128)(2,1)S(1)}, u32[]{:S(2)}, u32[]{:S(2)}) collective-permute-start(bf16[2,2,32,256]{3,2,1,0:T(8,128)(2,1)S(1)} %get-tuple-element.20), channel_id=1, source_target_pairs={{0,4},{2,6},{4,0},{6,2},{8,12},{10,14},{12,8},{14,10},{16,20},{18,... | collective-permute-start | bytes 196616 | tf_op jit(solution)/shard_map/cond/branch_0_fun/ppermute | solution.py:336
  15.9 4.5 %collective-permute-done.refs_0_ = bf16[2,2,32,256]{3,2,1,0:T(8,128)(2,1)S(1)} collective-permute-done((bf16[2,2,32,256]{3,2,1,0:T(8,128)(2,1)S(1)}, bf16[2,2,32,256]{3,2,1,0:T(8,128)(2,1)S(1)}, u32[]{:S(2)}, u32[]{:S(2)}) %collective-permute-start) | collective-permute-done | bytes 65568 | tf_op jit(solution)/shard_map/cond/branch_0_fun/ppermute | solution.py:336
  20.5 1.3 %collective-permute-done.2.refs_3_ = bf16[272,256]{1,0:T(8,128)(2,1)S(1)} collective-permute-done((bf16[272,256]{1,0:T(8,128)(2,1)S(1)}, bf16[272,256]{1,0:T(8,128)(2,1)S(1)}, u32[]{:S(2)}, u32[]{:S(2)}) %collective-permute-start.2) | collective-permute-done | bytes 139296 | tf_op jit(solution)/shard_map/cond/branch_0_fun/ppermute | solution.py:333
  21.8 0.3 scale.2
  22.1 0.1 collective-permute-start.3
  22.2 0.3 gram.2
  22.5 1.0 %collective-permute-done.3 = f32[4,32,256]{2,1,0:T(8,128)S(1)} collective-permute-done((f32[4,32,256]{2,1,0:T(8,128)S(1)}, f32[4,32,256]{2,1,0:T(8,128)S(1)}, u32[]{:S(2)}, u32[]{:S(2)}) %collective-permute-start.3) | collective-permute-done | bytes 131104 | tf_op jit(solution)/shard_map/cond/branch_0_fun/ppermute | solution.py:284
  23.6 0.9 %collective-permute-start.4 = (f32[1,32,256]{2,1,0:T(8,128)S(1)}, f32[1,32,256]{2,1,0:T(8,128)S(1)}, u32[]{:S(2)}, u32[]{:S(2)}) collective-permute-start(f32[1,32,256]{2,1,0:T(8,128)S(1)} %get-tuple-element.44), channel_id=1, source_target_pairs={{0,16},{2,18},{4,20},{6,22},{8,24},{10,26},{12,28},{14,30},{16,0},... | collective-permute-start | bytes 98312 | tf_op jit(solution)/shard_map/cond/branch_0_fun/ppermute | solution.py:301
  24.5 1.9 %collective-permute-start.5 = (f32[1,32,256]{2,1,0:T(8,128)S(1)}, f32[1,32,256]{2,1,0:T(8,128)S(1)}, u32[]{:S(2)}, u32[]{:S(2)}) collective-permute-start(f32[1,32,256]{2,1,0:T(8,128)S(1)} %get-tuple-element.46), channel_id=1, source_target_pairs={{0,24},{2,26},{4,28},{6,30},{8,16},{10,18},{12,20},{14,22},{16,8},... | collective-permute-start | bytes 98312 | tf_op jit(solution)/shard_map/cond/branch_0_fun/ppermute | solution.py:301
  26.4 0.7 %collective-permute-start.6 = (f32[1,32,256]{2,1,0:T(8,128)S(1)}, f32[1,32,256]{2,1,0:T(8,128)S(1)}, u32[]{:S(2)}, u32[]{:S(2)}) collective-permute-start(f32[1,32,256]{2,1,0:T(8,128)S(1)} %get-tuple-element.45), channel_id=1, source_target_pairs={{0,8},{2,10},{4,12},{6,14},{8,0},{10,2},{12,4},{14,6},{16,24},{18,... | collective-permute-start | bytes 98312 | tf_op jit(solution)/shard_map/cond/branch_0_fun/ppermute | solution.py:301
  27.1 2.3 %collective-permute-done.4 = f32[1,32,256]{2,1,0:T(8,128)S(1)} collective-permute-done((f32[1,32,256]{2,1,0:T(8,128)S(1)}, f32[1,32,256]{2,1,0:T(8,128)S(1)}, u32[]{:S(2)}, u32[]{:S(2)}) %collective-permute-start.4) | collective-permute-done | bytes 32800 | tf_op jit(solution)/shard_map/cond/branch_0_fun/ppermute | solution.py:301
  29.4 0.9 %collective-permute-done.5 = f32[1,32,256]{2,1,0:T(8,128)S(1)} collective-permute-done((f32[1,32,256]{2,1,0:T(8,128)S(1)}, f32[1,32,256]{2,1,0:T(8,128)S(1)}, u32[]{:S(2)}, u32[]{:S(2)}) %collective-permute-start.5) | collective-permute-done | bytes 32800 | tf_op jit(solution)/shard_map/cond/branch_0_fun/ppermute | solution.py:301
  30.2 0.3 %collective-permute-done.6 = f32[1,32,256]{2,1,0:T(8,128)S(1)} collective-permute-done((f32[1,32,256]{2,1,0:T(8,128)S(1)}, f32[1,32,256]{2,1,0:T(8,128)S(1)}, u32[]{:S(2)}, u32[]{:S(2)}) %collective-permute-start.6) | collective-permute-done | bytes 32800 | tf_op jit(solution)/shard_map/cond/branch_0_fun/ppermute | solution.py:301
  30.6 0.6 %broadcast_multiply_fusion = f32[32,256]{1,0:T(8,128)} fusion(f32[32,256]{1,0:T(8,128)S(1)} %get-tuple-element.50), kind=kLoop, calls=%fused_computation.8 | loop fusion | flops 8192 | bytes 65536 | tf_op jit(solution)/shard_map/mul | solution.py:280
  (14 shorter events, 0.1 us)
Async XLA Ops:
  0.0 9.5 %collective-permute-start.15 = (bf16[128,2,256]{2,1,0:T(2,128)(2,1)}, bf16[128,2,256]{2,1,0:T(2,128)(2,1)S(1)}, u32[]{:S(2)}, u32[]{:S(2)}) collective-permute-start(bf16[128,2,256]{2,1,0:T(2,128)(2,1)} %design_ref.1), channel_id=1, source_target_pairs={{0,24},{2,26},{4,12},{6,14},{8,0},{10,2},{12,20},{14,22},{16,8},{1... | collective-permute-start | bytes 393224 | tf_op jit(solution)/shard_map/ppermute | solution.py:234
  5.0 5.2 %collective-permute-start.16 = (bf16[128,2,256]{2,1,0:T(2,128)(2,1)}, bf16[128,2,256]{2,1,0:T(2,128)(2,1)S(1)}, u32[]{:S(2)}, u32[]{:S(2)}) collective-permute-start(bf16[128,2,256]{2,1,0:T(2,128)(2,1)} %design_ref.1), channel_id=1, source_target_pairs={{0,4},{2,6},{4,0},{6,2},{8,12},{10,14},{12,8},{14,10},{16,20},{18,... | collective-permute-start | bytes 393224 | tf_op jit(solution)/shard_map/ppermute | solution.py:245
  5.1 0.7 %copy-start.4 = (s32[128]{0:T(128)S(1)}, s32[128]{0:T(128)}, u32[]{:S(2)}) copy-start(s32[128]{0:T(128)} %param.10) | copy-start | bytes 1540
  5.1 0.7 %copy-start.2 = (f32[2,128]{1,0:T(2,128)S(1)}, f32[2,128]{1,0:T(2,128)}, u32[]{:S(2)}) copy-start(f32[2,128]{1,0:T(2,128)} %weights_ref.1) | copy-start | bytes 3076
  5.1 0.7 %copy-start.3 = (s32[128]{0:T(128)S(1)}, s32[128]{0:T(128)}, u32[]{:S(2)}) copy-start(s32[128]{0:T(128)} %param.11) | copy-start | bytes 1540
  5.8 3.7 %collective-permute-start.14 = (f32[8,128]{1,0:T(8,128)S(1)}, f32[8,128]{1,0:T(8,128)S(1)}, u32[]{:S(2)}, u32[]{:S(2)}) collective-permute-start(f32[8,128]{1,0:T(8,128)S(1)} %rows.1.rows_ref), channel_id=1, source_target_pairs={{0,24},{2,26},{4,12},{6,14},{8,0},{10,2},{12,4},{14,6},{16,8},{18,... | collective-permute-start | bytes 12296 | tf_op jit(solution)/shard_map/ppermute | solution.py:244
  7.5 0.9 %copy-start = (bf16[128,2,256]{2,1,0:T(2,128)(2,1)S(1)}, bf16[128,2,256]{2,1,0:T(2,128)(2,1)}, u32[]{:S(2)}) copy-start(bf16[128,2,256]{2,1,0:T(2,128)(2,1)} %design_ref.1) | copy-start | bytes 393220
  8.4 0.8 %copy-start.1 = (bf16[16,2,512]{2,1,0:T(2,128)(2,1)S(1)}, bf16[16,2,512]{2,1,0:T(2,128)(2,1)}, u32[]{:S(2)}) copy-start(bf16[16,2,512]{2,1,0:T(2,128)(2,1)} %taps_ref.1) | copy-start | bytes 98308
  10.3 0.7 %copy-start.5 = (s32[2]{0:T(128)S(1)}, s32[2]{0:T(128)}, u32[]{:S(2)}) copy-start(s32[2]{0:T(128)} %param.13) | copy-start | bytes 28
  10.3 1.6 %collective-permute-start.17 = (bf16[2,128,2,256]{3,2,1,0:T(2,128)(2,1)S(1)}, bf16[2,128,2,256]{3,2,1,0:T(2,128)(2,1)S(1)}, u32[]{:S(2)}, u32[]{:S(2)}) collective-permute-start(bf16[2,128,2,256]{3,2,1,0:T(2,128)(2,1)S(1)} %choose.1), channel_id=1, source_target_pairs={{0,2},{2,0},{4,6},{6,4},{8,10},{10,8},{12,14},{14,12},{16,18},{18,... | collective-permute-start | bytes 786440 | tf_op jit(solution)/shard_map/ppermute | solution.py:276
  12.4 8.1 %collective-permute-start.1 = (bf16[272,256]{1,0:T(8,128)(2,1)S(1)}, bf16[272,256]{1,0:T(8,128)(2,1)S(1)}, u32[]{:S(2)}, u32[]{:S(2)}) collective-permute-start(bf16[272,256]{1,0:T(8,128)(2,1)S(1)} %get-tuple-element.22), channel_id=1, source_target_pairs={{0,5},{1,4},{2,7},{3,6},{4,1},{5,0},{6,3},{7,2},{8,13},{9,12},{10,... | collective-permute-start | bytes 417800 | tf_op jit(solution)/shard_map/cond/branch_0_fun/ppermute | solution.py:334
  14.6 7.2 %collective-permute-start.2 = (bf16[272,256]{1,0:T(8,128)(2,1)S(1)}, bf16[272,256]{1,0:T(8,128)(2,1)S(1)}, u32[]{:S(2)}, u32[]{:S(2)}) collective-permute-start(bf16[272,256]{1,0:T(8,128)(2,1)S(1)} %get-tuple-element.22), channel_id=1, source_target_pairs={{0,1},{1,0},{2,3},{3,2},{4,5},{5,4},{6,7},{7,6},{8,9},{9,8},{10,11... | collective-permute-start | bytes 417800 | tf_op jit(solution)/shard_map/cond/branch_0_fun/ppermute | solution.py:333
  15.1 5.3 %collective-permute-start = (bf16[2,2,32,256]{3,2,1,0:T(8,128)(2,1)S(1)}, bf16[2,2,32,256]{3,2,1,0:T(8,128)(2,1)S(1)}, u32[]{:S(2)}, u32[]{:S(2)}) collective-permute-start(bf16[2,2,32,256]{3,2,1,0:T(8,128)(2,1)S(1)} %get-tuple-element.20), channel_id=1, source_target_pairs={{0,4},{2,6},{4,0},{6,2},{8,12},{10,14},{12,8},{14,10},{16,20},{18,... | collective-permute-start | bytes 196616 | tf_op jit(solution)/shard_map/cond/branch_0_fun/ppermute | solution.py:336
  22.1 1.4 %collective-permute-start.3 = (f32[4,32,256]{2,1,0:T(8,128)S(1)}, f32[4,32,256]{2,1,0:T(8,128)S(1)}, u32[]{:S(2)}, u32[]{:S(2)}) collective-permute-start(f32[4,32,256]{2,1,0:T(8,128)S(1)} %get-tuple-element.24), channel_id=1, source_target_pairs={{0,2},{2,0},{4,6},{6,4},{8,10},{10,8},{12,14},{14,12},{16,18},{18,... | collective-permute-start | bytes 393224 | tf_op jit(solution)/shard_map/cond/branch_0_fun/ppermute | solution.py:284
  23.6 5.8 %collective-permute-start.4 = (f32[1,32,256]{2,1,0:T(8,128)S(1)}, f32[1,32,256]{2,1,0:T(8,128)S(1)}, u32[]{:S(2)}, u32[]{:S(2)}) collective-permute-start(f32[1,32,256]{2,1,0:T(8,128)S(1)} %get-tuple-element.44), channel_id=1, source_target_pairs={{0,16},{2,18},{4,20},{6,22},{8,24},{10,26},{12,28},{14,30},{16,0},... | collective-permute-start | bytes 98312 | tf_op jit(solution)/shard_map/cond/branch_0_fun/ppermute | solution.py:301
  24.5 5.7 %collective-permute-start.5 = (f32[1,32,256]{2,1,0:T(8,128)S(1)}, f32[1,32,256]{2,1,0:T(8,128)S(1)}, u32[]{:S(2)}, u32[]{:S(2)}) collective-permute-start(f32[1,32,256]{2,1,0:T(8,128)S(1)} %get-tuple-element.46), channel_id=1, source_target_pairs={{0,24},{2,26},{4,28},{6,30},{8,16},{10,18},{12,20},{14,22},{16,8},... | collective-permute-start | bytes 98312 | tf_op jit(solution)/shard_map/cond/branch_0_fun/ppermute | solution.py:301
  26.4 4.2 %collective-permute-start.6 = (f32[1,32,256]{2,1,0:T(8,128)S(1)}, f32[1,32,256]{2,1,0:T(8,128)S(1)}, u32[]{:S(2)}, u32[]{:S(2)}) collective-permute-start(f32[1,32,256]{2,1,0:T(8,128)S(1)} %get-tuple-element.45), channel_id=1, source_target_pairs={{0,8},{2,10},{4,12},{6,14},{8,0},{10,2},{12,4},{14,6},{16,24},{18,... | collective-permute-start | bytes 98312 | tf_op jit(solution)/shard_map/cond/branch_0_fun/ppermute | solution.py:301
where the time goes:
time: 31.4 us; the launch traced here: 31.2 us
  starting transfers between devices  14.1 us (45%)
  waiting for transfers between devices  11.5 us (37%)
  local copies, waits for them, and re-layouts  2.94 us (9%)
  Pallas kernels  1.85 us (6%)
  other arithmetic  0.65 us (2%)
    ppermute x1, starting transfers between devices, body(): across = lax.ppermute(design, 'tm', across_pairs)  5.05 us
    ppermute x1, waiting for transfers between devices, run(): lax.ppermute(there, 'tm', beside_pairs)  4.53 us
    ppermute x3, starting transfers between devices, sum_over_groups(): lax.ppermute(share(place ^ d), 'tm', [(i, i ^ d * stride) for i in range(...  3.55 us
    ppermute x3, waiting for transfers between devices, sum_over_groups(): lax.ppermute(share(place ^ d), 'tm', [(i, i ^ d * stride) for i in range(...  3.44 us
    unnamed x12, local copies, waits for them, and re-layouts  2.92 us
    ppermute x1, starting transfers between devices, run(): lax.ppermute(every, ('tm', 'col'), both)  2.21 us
    ppermute x1, starting transfers between devices, body(): rows_across = lax.ppermute(rows, 'tm', rows_pairs)  1.78 us
    ppermute x1, waiting for transfers between devices, run(): lax.ppermute(every, 'col', across_column)  1.33 us
  transfers between devices with their start and end apart: 11, of which 8 were waited for; matrix products, arithmetic and copies ran while one was open for 0% of the time, Pallas kernels for 3%

commit v1 on v0

--- a/solution.py
+++ b/solution.py
@@ -11,9 +11,11 @@
 SMEM = pl.BlockSpec(memory_space=pltpu.SMEM)
 FIRST = (((0,), (0,)), ((), ()))
 LIMIT = pltpu.CompilerParams(vmem_limit_bytes=24 * 2**20)
-
-
-def rows_kernel(weights_ref, flags_ref, segment_ref, rows_ref):
+LONG = pl.CostEstimate(flops=2 * 10**10, bytes_accessed=2**20, transcendentals=0)
+
+
+def rows_kernel(weights_ref, flags_ref, segment_ref, ids_ref, rows_ref, ids_out_ref):
+    ids_out_ref[...] = ids_ref[...]
     rows_ref[0:2, :] = weights_ref[...] * flags_ref[...].astype(jnp.float32)
     rows_ref[2:3, :] = segment_ref[...].astype(jnp.float32)
     rows_ref[3:, :] = jnp.zeros_like(rows_ref[3:, :])
@@ -40,7 +42,7 @@
     spread_ref[...] = spread.astype(jnp.bfloat16)
 
 
-def choose_kernel(rows_across_ref, across_ref, own_ref, beside_ref, out_ref):
+def choose_kernel(across_ref, own_ref, beside_ref, out_ref):
     out_ref[1] = beside_ref[...]
     index = lax.axis_index("tm")
     both = jnp.bitwise_and(jnp.bitwise_xor(index, lax.div(index, 2)), 1)
@@ -108,7 +110,7 @@
 
 
 def filter_split_kernel(
-    toeplitz_ref, across_ref, own_ref, beside_ref, swapped_ref, rows_ref, all_ref, here_ref, there_ref
+    toeplitz_ref, beside_ref, own_ref, across_ref, swapped_ref, rows_ref, all_ref, here_ref, there_ref
 ):
     block = filtered_block(toeplitz_ref, across_ref, own_ref, beside_ref, swapped_ref)
     width, length = block.shape
@@ -131,9 +133,9 @@
             there_ref[...] = block[:, 1 - side]
 
 
-def split_scale_kernel(*refs):
+def split_scale_kernel(back, *refs):
     *held_refs, other_ref, scaled_ref = refs
-    held_refs = [held_refs[i] for i in (3, 2, 1, 0)]
+    held_refs = [held_refs[i] for i in back]
     width = scaled_ref.shape[1]
     for unit, ref in enumerate(held_refs[:2]):
         lines = ref[width:, :].astype(jnp.float32)
@@ -142,9 +144,9 @@
     split_gram(held_refs, scaled_ref, other_ref, 1)
 
 
-def split_gram_kernel(scaled_ref, *refs):
+def split_gram_kernel(back, scaled_ref, *refs):
     *held_refs, mine_ref = refs
-    held_refs = [held_refs[i] for i in (3, 2, 1, 0)]
+    held_refs = [held_refs[i] for i in back]
     split_gram(held_refs, scaled_ref, mine_ref, 0)
 
 
@@ -232,14 +234,17 @@
     across_pairs = [(i, (i + (4 if i & 2 else -4)) % devices) for i in range(devices)]
 
     across = lax.ppermute(design, "tm", across_pairs)
-    rows = pl.pallas_call(
+    rows, ids = pl.pallas_call(
         rows_kernel,
-        out_shape=jax.ShapeDtypeStruct((8, row_count), jnp.float32),
-        in_specs=[VMEM] * 3,
-        out_specs=VMEM,
+        out_shape=[
+            jax.ShapeDtypeStruct((8, row_count), jnp.float32),
+            jax.ShapeDtypeStruct((1, columns), jnp.int32),
+        ],
+        in_specs=[VMEM] * 4,
+        out_specs=[VMEM] * 2,
         compiler_params=LIMIT,
         name="rows",
-    )(weights, valid_flags.reshape(1, row_count), segment.reshape(1, row_count))
+    )(weights, valid_flags.reshape(1, row_count), segment.reshape(1, row_count), block_ids.reshape(1, columns))
     rows_pairs = [(i, i ^ 4 if i & 2 else (i - 4) % devices) for i in range(devices)]
     rows_across = lax.ppermute(rows, "tm", rows_pairs)
     beside = lax.ppermute(design, "tm", beside_pairs)
@@ -263,20 +268,21 @@
         in_specs=[VMEM] * 3,
         out_specs=[VMEM] * 2,
         compiler_params=LIMIT,
+        cost_estimate=LONG,
         name="toeplitz",
     )(rows, rows_across, spread)
     chosen = pl.pallas_call(
         choose_kernel,
         out_shape=jax.ShapeDtypeStruct((2, *design.shape), design.dtype),
-        in_specs=[VMEM] * 4,
+        in_specs=[VMEM] * 3,
         out_specs=VMEM,
         compiler_params=LIMIT,
         name="choose",
-    )(rows_across, across, own, beside)
+    )(across, own, beside)
     swapped = lax.ppermute(chosen, "tm", swap)
     split = columns == 2 and rows_out % 16 == 0 and block_width % (4 * rows_out) == 0
     finish = finish_two if split else finish_any
-    total = finish(toeplitz, rows_here, (across, own, beside, swapped), block_ids, rows_out, swap, beside_pairs)
+    total = finish(toeplitz, rows_here, (across, own, beside, swapped), ids.reshape(columns), rows_out, swap, beside_pairs)
     return total * (1.0 / (2.0 * row_count * devices))
 
 
@@ -297,7 +303,7 @@
             return lax.dynamic_index_in_dim(shares, j, 1, keepdims=False)
 
         total = share(place)
-        for d in (2, 3, 1)[-(group - 1) :]:
+        for d in ((3, 1, 2) if group == 4 else (1,)):
             total = total + lax.ppermute(share(place ^ d), "tm", [(i, i ^ (d * stride)) for i in range(devices)])
         stride, left = stride * group, left // group
     return total[0]
@@ -315,7 +321,7 @@
         out_specs=[VMEM] * 3,
         compiler_params=LIMIT,
         name="filter",
-    )(toeplitz, *blocks, rows_here)
+    )(toeplitz, blocks[2], blocks[1], blocks[0], blocks[3], rows_here)
 
     def sums(own_block):
         def run(every, here, there):
@@ -335,23 +341,25 @@
                     here,
                     lax.ppermute(there, "tm", beside_pairs),
                 )
+            order = (1, 3, 2, 0) if own_block else (3, 0, 1, 2)
+            back = tuple(order.index(i) for i in range(4))
             share = jax.ShapeDtypeStruct((2 * groups, rows_out, width), jnp.float32)
             other, scaled = pl.pallas_call(
-                split_scale_kernel,
+                functools.partial(split_scale_kernel, back),
                 out_shape=[share, jax.ShapeDtypeStruct((2, width, length), jnp.bfloat16)],
                 in_specs=[VMEM] * 4,
                 out_specs=[VMEM] * 2,
                 compiler_params=LIMIT,
                 name="scale",
-            )(*(held[i] for i in (3, 2, 1, 0)))
+            )(*(held[i] for i in order))
             mine = pl.pallas_call(
-                split_gram_kernel,
+                functools.partial(split_gram_kernel, back),
                 out_shape=share,
                 in_specs=[VMEM] * 5,
                 out_specs=VMEM,
                 compiler_params=LIMIT,
                 name="gram",
-            )(scaled, *(held[i] for i in (3, 2, 1, 0)))
+            )(scaled, *(held[i] for i in order))
             return sum_over_groups(core_sum(mine, other, swap), 4)
 
         return run

time: 31.4 us -> 30 us (0.955); the launches traced: 31.2 us -> 30.5 us
  waiting for transfers between devices: 11.5 us -> 10.4 us
  starting transfers between devices: 14.1 us -> 15 us
  local copies, waits for them, and re-layouts: 2.94 us -> 2.37 us
    ppermute x1, starting transfers between devices: 0.81 us -> 1.72 us  [run(): lax.ppermute(there, 'tm', beside_pairs)]
    ppermute x1, starting transfers between devices: 2.21 us -> 1.3 us  [run(): lax.ppermute(every, ('tm', 'col'), both)]
    ppermute x3, starting transfers between devices: 3.55 us -> 4.45 us  [sum_over_groups(): lax.ppermute(share(place ^ d), 'tm', [(i, i ^ d * stride) for i in range(...]
    ppermute x1, waiting for transfers between devices: 1.33 us -> 0.43 us  [run(): lax.ppermute(every, 'col', across_column)]
    ppermute x3, waiting for transfers between devices: 3.44 us -> 2.72 us  [sum_over_groups(): lax.ppermute(share(place ^ d), 'tm', [(i, i ^ d * stride) for i in range(...]
    ppermute x1, waiting for transfers between devices: 0.42 us -> 1.02 us  [body(): swapped = lax.ppermute(chosen, 'tm', swap)]
    unnamed x12, local copies, waits for them, and re-layouts: 2.92 us -> 2.36 us
  transfers between devices with their start and end apart: 11 -> 11, of which waited for: 8 -> 7; matrix products, arithmetic and copies ran while one was open for 0% -> 0% of each run, Pallas kernels for 3% -> 4%
where the time goes in v1:
time: 30 us; the launch traced here: 30.5 us
  starting transfers between devices  15 us (50%)
  waiting for transfers between devices  10.4 us (35%)
  local copies, waits for them, and re-layouts  2.37 us (8%)
  Pallas kernels  1.85 us (6%)
  other arithmetic  0.65 us (2%)
    ppermute x1, starting transfers between devices, body(): across = lax.ppermute(design, 'tm', across_pairs)  5.05 us
    ppermute x1, waiting for transfers between devices, run(): lax.ppermute(there, 'tm', beside_pairs)  4.53 us
    ppermute x3, starting transfers between devices, sum_over_groups(): lax.ppermute(share(place ^ d), 'tm', [(i, i ^ d * stride) for i in range(...  4.45 us
    ppermute x3, waiting for transfers between devices, sum_over_groups(): lax.ppermute(share(place ^ d), 'tm', [(i, i ^ d * stride) for i in range(...  2.72 us
    unnamed x12, local copies, waits for them, and re-layouts  2.36 us
    ppermute x1, starting transfers between devices, body(): rows_across = lax.ppermute(rows, 'tm', rows_pairs)  1.79 us
    ppermute x1, starting transfers between devices, run(): lax.ppermute(there, 'tm', beside_pairs)  1.72 us
    ppermute x1, starting transfers between devices, run(): lax.ppermute(every, ('tm', 'col'), both)  1.3 us
  transfers between devices with their start and end apart: 11, of which 7 were waited for; matrix products, arithmetic and copies ran while one was open for 0% of the time, Pallas kernels for 4%

profile of v1, /device:TPU:0, one launch (start us, length us, event | category | flops | bytes accessed | tf_op | source)
XLA Modules:
  0.0 30.5 jit_solution(2196725153197700128)
XLA Ops:
  0.0 5.0 %collective-permute-start.16 = (bf16[128,2,256]{2,1,0:T(2,128)(2,1)}, bf16[128,2,256]{2,1,0:T(2,128)(2,1)S(1)}, u32[]{:S(2)}, u32[]{:S(2)}) collective-permute-start(bf16[128,2,256]{2,1,0:T(2,128)(2,1)} %design_ref.1), channel_id=1, source_target_pairs={{0,24},{2,26},{4,12},{6,14},{8,0},{10,2},{12,20},{14,22},{16,8},{1... | collective-permute-start | bytes 393224 | tf_op jit(solution)/shard_map/ppermute | solution.py:236
  5.0 0.0 collective-permute-start.15
  5.1 0.6 %copy-done.4 = s32[128]{0:T(128)S(1)} copy-done((s32[128]{0:T(128)S(1)}, s32[128]{0:T(128)}, u32[]{:S(2)}) %copy-start.4) | copy-done | bytes 536
  5.7 0.0 copy-done.5
  5.7 0.0 copy-done.2
  5.8 1.8 %collective-permute-start.14 = (f32[8,128]{1,0:T(8,128)S(1)}, f32[8,128]{1,0:T(8,128)S(1)}, u32[]{:S(2)}, u32[]{:S(2)}) collective-permute-start(f32[8,128]{1,0:T(8,128)S(1)} %get-tuple-element.40.rows_ref), channel_id=1, source_target_pairs={{0,24},{2,26},{4,12},{6,14},{8,0},{10,2},{12,4},{14,6},{16,8},{18,... | collective-permute-start | bytes 12296 | tf_op jit(solution)/shard_map/ppermute | solution.py:249
  7.6 0.0 copy-start
  7.6 0.9 %copy-done = bf16[128,2,256]{2,1,0:T(2,128)(2,1)S(1)} copy-done((bf16[128,2,256]{2,1,0:T(2,128)(2,1)S(1)}, bf16[128,2,256]{2,1,0:T(2,128)(2,1)}, u32[]{:S(2)}) %copy-start) | copy-done | bytes 131096
  8.5 0.8 %copy-done.1 = bf16[16,2,512]{2,1,0:T(2,128)(2,1)S(1)} copy-done((bf16[16,2,512]{2,1,0:T(2,128)(2,1)S(1)}, bf16[16,2,512]{2,1,0:T(2,128)(2,1)}, u32[]{:S(2)}) %copy-start.1) | copy-done | bytes 32792
  9.3 0.3 prepare.1
  9.6 0.7 %collective-permute-done.15.beside_ref = bf16[128,2,256]{2,1,0:T(2,128)(2,1)S(1)} collective-permute-done((bf16[128,2,256]{2,1,0:T(2,128)(2,1)}, bf16[128,2,256]{2,1,0:T(2,128)(2,1)S(1)}, u32[]{:S(2)}, u32[]{:S(2)}) %collective-permute-start.15) | collective-permute-done | bytes 131104 | tf_op jit(solution)/shard_map/ppermute | solution.py:250
  10.3 0.1 collective-permute-start.17
  10.3 0.5 %toeplitz.1 = (bf16[5,256,256]{2,1,0:T(8,128)(2,1)S(1)}, f32[8,128]{1,0:T(8,128)S(1)}) custom-call(f32[8,128]{1,0:T(8,128)S(1)} %get-tuple-element.40.rows_ref, f32[8,128]{1,0:T(8,128)S(1)} %collective-permute-done.14.rows_across_ref, bf16[32,1280]{1,0:T(8,128)(2,1)S(1)} %get-tuple-element.41.spread_ref), custom_call_target="tpu_custom_call" | custom-call | flops 20000000000 | bytes 1048576 | tf_op jit(solution)/shard_map/toeplitz/pallas_call | solution.py:262
  10.8 1.0 %collective-permute-done.17.swapped_ref = bf16[2,128,2,256]{3,2,1,0:T(2,128)(2,1)S(1)} collective-permute-done((bf16[2,128,2,256]{3,2,1,0:T(2,128)(2,1)S(1)}, bf16[2,128,2,256]{3,2,1,0:T(2,128)(2,1)S(1)}, u32[]{:S(2)}, u32[]{:S(2)}) %collective-permute-start.17) | collective-permute-done | bytes 262176 | tf_op jit(solution)/shard_map/ppermute | solution.py:282
  11.9 0.5 %filter.1 = (bf16[272,256]{1,0:T(8,128)(2,1)S(1)}, bf16[2,2,32,256]{3,2,1,0:T(8,128)(2,1)S(1)}, bf16[2,2,32,256]{3,2,1,0:T(8,128)(2,1)S(1)}) custom-call(bf16[5,256,256]{2,1,0:T(8,128)(2,1)S(1)} %get-tuple-element.42.toeplitz_ref, bf16[128,2,256]{2,1,0:T(2,128)(2,1)S(1)} %collective-permute-done.15.beside_ref, ...), custom_call_target="tpu_custom_call" | custom-call | tf_op jit(solution)/shard_map/filter/pallas_call | solution.py:317
  12.4 17.5 %conditional.1 = (f32[32,256]{1,0:T(8,128)S(1)}) conditional(s32[]{:T(128)} %bitcast.5, (bf16[2,2,32,256]{3,2,1,0:T(8,128)(2,1)S(1)}, bf16[272,256]{1,0:T(8,128)(2,1)S(1)}, bf16[2,2,32,256]{3,2,1,0:T(8,128)(2,1)S(1)}) %tuple.11, (bf16[272,256]{1,0:T(8,128)(2,1)S(1)}, bf16[2,2,32,256]{3,2,1,0:T(8,128)(2,1)S(1)}, ...), branch_computations={%region_0.1_spmd, %region_1.2_spmd} | conditional | flops 57388 | bytes 3048191 | solution.py:367
  12.4 1.3 %collective-permute-start.2 = (bf16[272,256]{1,0:T(8,128)(2,1)S(1)}, bf16[272,256]{1,0:T(8,128)(2,1)S(1)}, u32[]{:S(2)}, u32[]{:S(2)}) collective-permute-start(bf16[272,256]{1,0:T(8,128)(2,1)S(1)} %get-tuple-element.21), channel_id=1, source_target_pairs={{0,5},{1,4},{2,7},{3,6},{4,1},{5,0},{6,3},{7,2},{8,13},{9,12},{10,... | collective-permute-start | bytes 417800 | tf_op jit(solution)/shard_map/cond/branch_0_fun/ppermute | solution.py:340
  13.7 0.5 %collective-permute-start.1 = (bf16[272,256]{1,0:T(8,128)(2,1)S(1)}, bf16[272,256]{1,0:T(8,128)(2,1)S(1)}, u32[]{:S(2)}, u32[]{:S(2)}) collective-permute-start(bf16[272,256]{1,0:T(8,128)(2,1)S(1)} %get-tuple-element.21), channel_id=1, source_target_pairs={{0,1},{1,0},{2,3},{3,2},{4,5},{5,4},{6,7},{7,6},{8,9},{9,8},{10,11... | collective-permute-start | bytes 417800 | tf_op jit(solution)/shard_map/cond/branch_0_fun/ppermute | solution.py:339
  14.2 1.7 %collective-permute-start = (bf16[2,2,32,256]{3,2,1,0:T(8,128)(2,1)S(1)}, bf16[2,2,32,256]{3,2,1,0:T(8,128)(2,1)S(1)}, u32[]{:S(2)}, u32[]{:S(2)}) collective-permute-start(bf16[2,2,32,256]{3,2,1,0:T(8,128)(2,1)S(1)} %get-tuple-element.20), channel_id=1, source_target_pairs={{0,4},{2,6},{4,0},{6,2},{8,12},{10,14},{12,8},{14,10},{16,20},{18,... | collective-permute-start | bytes 196616 | tf_op jit(solution)/shard_map/cond/branch_0_fun/ppermute | solution.py:342
  15.9 4.5 %collective-permute-done.refs_0_ = bf16[2,2,32,256]{3,2,1,0:T(8,128)(2,1)S(1)} collective-permute-done((bf16[2,2,32,256]{3,2,1,0:T(8,128)(2,1)S(1)}, bf16[2,2,32,256]{3,2,1,0:T(8,128)(2,1)S(1)}, u32[]{:S(2)}, u32[]{:S(2)}) %collective-permute-start) | collective-permute-done | bytes 65568 | tf_op jit(solution)/shard_map/cond/branch_0_fun/ppermute | solution.py:342
  20.5 0.4 %collective-permute-done.1.refs_1_ = bf16[272,256]{1,0:T(8,128)(2,1)S(1)} collective-permute-done((bf16[272,256]{1,0:T(8,128)(2,1)S(1)}, bf16[272,256]{1,0:T(8,128)(2,1)S(1)}, u32[]{:S(2)}, u32[]{:S(2)}) %collective-permute-start.1) | collective-permute-done | bytes 139296 | tf_op jit(solution)/shard_map/cond/branch_0_fun/ppermute | solution.py:339
  20.9 0.3 scale.2
  21.2 0.1 collective-permute-start.3
  21.3 0.3 gram.2
  21.6 1.0 %collective-permute-done.3 = f32[4,32,256]{2,1,0:T(8,128)S(1)} collective-permute-done((f32[4,32,256]{2,1,0:T(8,128)S(1)}, f32[4,32,256]{2,1,0:T(8,128)S(1)}, u32[]{:S(2)}, u32[]{:S(2)}) %collective-permute-start.3) | collective-permute-done | bytes 131104 | tf_op jit(solution)/shard_map/cond/branch_0_fun/ppermute | solution.py:290
  22.6 2.2 %collective-permute-start.4 = (f32[1,32,256]{2,1,0:T(8,128)S(1)}, f32[1,32,256]{2,1,0:T(8,128)S(1)}, u32[]{:S(2)}, u32[]{:S(2)}) collective-permute-start(f32[1,32,256]{2,1,0:T(8,128)S(1)} %get-tuple-element.48), channel_id=1, source_target_pairs={{0,24},{2,26},{4,28},{6,30},{8,16},{10,18},{12,20},{14,22},{16,8},... | collective-permute-start | bytes 98312 | tf_op jit(solution)/shard_map/cond/branch_0_fun/ppermute | solution.py:307
  24.8 0.7 %collective-permute-start.6 = (f32[1,32,256]{2,1,0:T(8,128)S(1)}, f32[1,32,256]{2,1,0:T(8,128)S(1)}, u32[]{:S(2)}, u32[]{:S(2)}) collective-permute-start(f32[1,32,256]{2,1,0:T(8,128)S(1)} %get-tuple-element.49), channel_id=1, source_target_pairs={{0,16},{2,18},{4,20},{6,22},{8,24},{10,26},{12,28},{14,30},{16,0},... | collective-permute-start | bytes 98312 | tf_op jit(solution)/shard_map/cond/branch_0_fun/ppermute | solution.py:307
  25.6 1.5 %collective-permute-start.5 = (f32[1,32,256]{2,1,0:T(8,128)S(1)}, f32[1,32,256]{2,1,0:T(8,128)S(1)}, u32[]{:S(2)}, u32[]{:S(2)}) collective-permute-start(f32[1,32,256]{2,1,0:T(8,128)S(1)} %get-tuple-element.50), channel_id=1, source_target_pairs={{0,8},{2,10},{4,12},{6,14},{8,0},{10,2},{12,4},{14,6},{16,24},{18,... | collective-permute-start | bytes 98312 | tf_op jit(solution)/shard_map/cond/branch_0_fun/ppermute | solution.py:307
  27.1 1.5 %collective-permute-done.4 = f32[1,32,256]{2,1,0:T(8,128)S(1)} collective-permute-done((f32[1,32,256]{2,1,0:T(8,128)S(1)}, f32[1,32,256]{2,1,0:T(8,128)S(1)}, u32[]{:S(2)}, u32[]{:S(2)}) %collective-permute-start.4) | collective-permute-done | bytes 32800 | tf_op jit(solution)/shard_map/cond/branch_0_fun/ppermute | solution.py:307
  28.6 1.2 %collective-permute-done.6 = f32[1,32,256]{2,1,0:T(8,128)S(1)} collective-permute-done((f32[1,32,256]{2,1,0:T(8,128)S(1)}, f32[1,32,256]{2,1,0:T(8,128)S(1)}, u32[]{:S(2)}, u32[]{:S(2)}) %collective-permute-start.6) | collective-permute-done | bytes 32800 | tf_op jit(solution)/shard_map/cond/branch_0_fun/ppermute | solution.py:307
  29.8 0.0 collective-permute-done.5
  29.8 0.6 %broadcast_multiply_fusion = f32[32,256]{1,0:T(8,128)} fusion(f32[32,256]{1,0:T(8,128)S(1)} %get-tuple-element.54), kind=kLoop, calls=%fused_computation.8 | loop fusion | flops 8192 | bytes 65536 | tf_op jit(solution)/shard_map/mul | solution.py:286
  (14 shorter events, 0.1 us)
Async XLA Ops:
  0.0 9.6 %collective-permute-start.16 = (bf16[128,2,256]{2,1,0:T(2,128)(2,1)}, bf16[128,2,256]{2,1,0:T(2,128)(2,1)S(1)}, u32[]{:S(2)}, u32[]{:S(2)}) collective-permute-start(bf16[128,2,256]{2,1,0:T(2,128)(2,1)} %design_ref.1), channel_id=1, source_target_pairs={{0,24},{2,26},{4,12},{6,14},{8,0},{10,2},{12,20},{14,22},{16,8},{1... | collective-permute-start | bytes 393224 | tf_op jit(solution)/shard_map/ppermute | solution.py:236
  5.0 5.2 %collective-permute-start.15 = (bf16[128,2,256]{2,1,0:T(2,128)(2,1)}, bf16[128,2,256]{2,1,0:T(2,128)(2,1)S(1)}, u32[]{:S(2)}, u32[]{:S(2)}) collective-permute-start(bf16[128,2,256]{2,1,0:T(2,128)(2,1)} %design_ref.1), channel_id=1, source_target_pairs={{0,4},{2,6},{4,0},{6,2},{8,12},{10,14},{12,8},{14,10},{16,20},{18,... | collective-permute-start | bytes 393224 | tf_op jit(solution)/shard_map/ppermute | solution.py:250
  5.1 0.7 %copy-start.4 = (s32[128]{0:T(128)S(1)}, s32[128]{0:T(128)}, u32[]{:S(2)}) copy-start(s32[128]{0:T(128)} %param.10) | copy-start | bytes 1540
  5.1 0.7 %copy-start.5 = (s32[2]{0:T(128)S(1)}, s32[2]{0:T(128)}, u32[]{:S(2)}) copy-start(s32[2]{0:T(128)} %param.13) | copy-start | bytes 28
  5.1 0.7 %copy-start.2 = (f32[2,128]{1,0:T(2,128)S(1)}, f32[2,128]{1,0:T(2,128)}, u32[]{:S(2)}) copy-start(f32[2,128]{1,0:T(2,128)} %weights_ref.1) | copy-start | bytes 3076
  5.1 0.7 %copy-start.3 = (s32[128]{0:T(128)S(1)}, s32[128]{0:T(128)}, u32[]{:S(2)}) copy-start(s32[128]{0:T(128)} %param.11) | copy-start | bytes 1540
  5.8 4.6 %collective-permute-start.14 = (f32[8,128]{1,0:T(8,128)S(1)}, f32[8,128]{1,0:T(8,128)S(1)}, u32[]{:S(2)}, u32[]{:S(2)}) collective-permute-start(f32[8,128]{1,0:T(8,128)S(1)} %get-tuple-element.40.rows_ref), channel_id=1, source_target_pairs={{0,24},{2,26},{4,12},{6,14},{8,0},{10,2},{12,4},{14,6},{16,8},{18,... | collective-permute-start | bytes 12296 | tf_op jit(solution)/shard_map/ppermute | solution.py:249
  7.6 0.9 %copy-start = (bf16[128,2,256]{2,1,0:T(2,128)(2,1)S(1)}, bf16[128,2,256]{2,1,0:T(2,128)(2,1)}, u32[]{:S(2)}) copy-start(bf16[128,2,256]{2,1,0:T(2,128)(2,1)} %design_ref.1) | copy-start | bytes 393220
  8.5 0.8 %copy-start.1 = (bf16[16,2,512]{2,1,0:T(2,128)(2,1)S(1)}, bf16[16,2,512]{2,1,0:T(2,128)(2,1)}, u32[]{:S(2)}) copy-start(bf16[16,2,512]{2,1,0:T(2,128)(2,1)} %taps_ref.1) | copy-start | bytes 98308
  10.3 1.6 %collective-permute-start.17 = (bf16[2,128,2,256]{3,2,1,0:T(2,128)(2,1)S(1)}, bf16[2,128,2,256]{3,2,1,0:T(2,128)(2,1)S(1)}, u32[]{:S(2)}, u32[]{:S(2)}) collective-permute-start(bf16[2,128,2,256]{3,2,1,0:T(2,128)(2,1)S(1)} %choose.1), channel_id=1, source_target_pairs={{0,2},{2,0},{4,6},{6,4},{8,10},{10,8},{12,14},{14,12},{16,18},{18,... | collective-permute-start | bytes 786440 | tf_op jit(solution)/shard_map/ppermute | solution.py:282
  12.4 8.1 %collective-permute-start.2 = (bf16[272,256]{1,0:T(8,128)(2,1)S(1)}, bf16[272,256]{1,0:T(8,128)(2,1)S(1)}, u32[]{:S(2)}, u32[]{:S(2)}) collective-permute-start(bf16[272,256]{1,0:T(8,128)(2,1)S(1)} %get-tuple-element.21), channel_id=1, source_target_pairs={{0,5},{1,4},{2,7},{3,6},{4,1},{5,0},{6,3},{7,2},{8,13},{9,12},{10,... | collective-permute-start | bytes 417800 | tf_op jit(solution)/shard_map/cond/branch_0_fun/ppermute | solution.py:340
  13.7 7.2 %collective-permute-start.1 = (bf16[272,256]{1,0:T(8,128)(2,1)S(1)}, bf16[272,256]{1,0:T(8,128)(2,1)S(1)}, u32[]{:S(2)}, u32[]{:S(2)}) collective-permute-start(bf16[272,256]{1,0:T(8,128)(2,1)S(1)} %get-tuple-element.21), channel_id=1, source_target_pairs={{0,1},{1,0},{2,3},{3,2},{4,5},{5,4},{6,7},{7,6},{8,9},{9,8},{10,11... | collective-permute-start | bytes 417800 | tf_op jit(solution)/shard_map/cond/branch_0_fun/ppermute | solution.py:339
  14.2 6.2 %collective-permute-start = (bf16[2,2,32,256]{3,2,1,0:T(8,128)(2,1)S(1)}, bf16[2,2,32,256]{3,2,1,0:T(8,128)(2,1)S(1)}, u32[]{:S(2)}, u32[]{:S(2)}) collective-permute-start(bf16[2,2,32,256]{3,2,1,0:T(8,128)(2,1)S(1)} %get-tuple-element.20), channel_id=1, source_target_pairs={{0,4},{2,6},{4,0},{6,2},{8,12},{10,14},{12,8},{14,10},{16,20},{18,... | collective-permute-start | bytes 196616 | tf_op jit(solution)/shard_map/cond/branch_0_fun/ppermute | solution.py:342
  21.2 1.4 %collective-permute-start.3 = (f32[4,32,256]{2,1,0:T(8,128)S(1)}, f32[4,32,256]{2,1,0:T(8,128)S(1)}, u32[]{:S(2)}, u32[]{:S(2)}) collective-permute-start(f32[4,32,256]{2,1,0:T(8,128)S(1)} %get-tuple-element.24), channel_id=1, source_target_pairs={{0,2},{2,0},{4,6},{6,4},{8,10},{10,8},{12,14},{14,12},{16,18},{18,... | collective-permute-start | bytes 393224 | tf_op jit(solution)/shard_map/cond/branch_0_fun/ppermute | solution.py:290
  22.6 5.9 %collective-permute-start.4 = (f32[1,32,256]{2,1,0:T(8,128)S(1)}, f32[1,32,256]{2,1,0:T(8,128)S(1)}, u32[]{:S(2)}, u32[]{:S(2)}) collective-permute-start(f32[1,32,256]{2,1,0:T(8,128)S(1)} %get-tuple-element.48), channel_id=1, source_target_pairs={{0,24},{2,26},{4,28},{6,30},{8,16},{10,18},{12,20},{14,22},{16,8},... | collective-permute-start | bytes 98312 | tf_op jit(solution)/shard_map/cond/branch_0_fun/ppermute | solution.py:307
  24.8 5.0 %collective-permute-start.6 = (f32[1,32,256]{2,1,0:T(8,128)S(1)}, f32[1,32,256]{2,1,0:T(8,128)S(1)}, u32[]{:S(2)}, u32[]{:S(2)}) collective-permute-start(f32[1,32,256]{2,1,0:T(8,128)S(1)} %get-tuple-element.49), channel_id=1, source_target_pairs={{0,16},{2,18},{4,20},{6,22},{8,24},{10,26},{12,28},{14,30},{16,0},... | collective-permute-start | bytes 98312 | tf_op jit(solution)/shard_map/cond/branch_0_fun/ppermute | solution.py:307
  25.6 4.3 %collective-permute-start.5 = (f32[1,32,256]{2,1,0:T(8,128)S(1)}, f32[1,32,256]{2,1,0:T(8,128)S(1)}, u32[]{:S(2)}, u32[]{:S(2)}) collective-permute-start(f32[1,32,256]{2,1,0:T(8,128)S(1)} %get-tuple-element.50), channel_id=1, source_target_pairs={{0,8},{2,10},{4,12},{6,14},{8,0},{10,2},{12,4},{14,6},{16,24},{18,... | collective-permute-start | bytes 98312 | tf_op jit(solution)/shard_map/cond/branch_0_fun/ppermute | solution.py:307
